TPU v7x, 256 devices: a whole 4x4x8 slice. The times are simulated.
256 devices in a mesh: seq: 32 (over x, y, core), head: 8 (over z).
Axes of the slice: x: 4, y: 4, z: 8, core: 2. Of those that a mesh axis runs over, the one named last changes fastest.
Arguments:
- residual: bfloat16 [16384, 4096], P(('seq', 'head')), may hold values from -6 to 6
- sliding_query_heads: bfloat16 [16384, 4096], P('seq', 'head'), may hold values from -64 to 64
- sliding_key_heads: bfloat16 [16384, 1024], P('seq', 'head'), may hold values from -6 to 6
- sliding_value_heads: bfloat16 [16384, 1024], P('seq', 'head'), may hold values from -6 to 6
- output_weight: bfloat16 [4096, 4096], P('head'), may hold values from -0.5 to 0.5
- norm_gain: float32 [4096], replicated, may hold values from 0.5 to 1.5
- query_weight: bfloat16 [4096, 1024], P(None, 'head'), may hold values from -0.09375 to 0.09375
- key_weight: bfloat16 [4096, 1024], P(None, 'head'), may hold values from -0.09375 to 0.09375
- value_weight: bfloat16 [4096, 4096], P(None, 'head'), may hold values from -0.09375 to 0.09375
- write_strength: float32 [32, 16384], P('head', 'seq'), may hold values from 0.0029 to 0.301
- log_decay: float32 [32, 16384], P('head', 'seq'), may hold values from -2 to 0
Outputs:
- mixed_stream: bfloat16 [16384, 4096], P(('seq', 'head'))
- delta_output: bfloat16 [16384, 4096], P('seq', 'head')
All inputs are finite; a program needn't handle non-finite values.
Results may differ from a plain program's by a relative error of at most 0.024.
Values may be sent and summed in bfloat16 or wider, within the bound.
No kernel may reach another device: no remote copies, remote signals or barrier semaphores. Data moves between devices by JAX's collectives and lax.ppermute only.
A program may use at most 128 MiB of HBM per device.

v0:
```python
import math

import jax
import jax.numpy as jnp
from jax import lax
from jax.sharding import PartitionSpec as P

QUERY_HEADS = 32
KEY_VALUE_HEADS = 8
HK = 8
DELTA_VALUE_HEADS = 32
HEAD_WIDTH = 128
WINDOW_KEYS = 4096
CH = 64


precise = lax.Precision.HIGHEST


def shifted(x, axis, by):
    count = lax.axis_size(axis)
    pairs = [(i, i + by) for i in range(count) if 0 <= i + by < count]
    return lax.ppermute(x, axis, pairs)


def carried_in(x, axis, combine, identity):
    count, index = (lax.axis_size(axis), lax.axis_index(axis))
    everything = jax.tree.map(
        lambda part, kind: lax.all_gather(part.astype(kind), axis), x, (jnp.bfloat16, jnp.bfloat16)
    )
    start = jax.tree.map(
        lambda part, zero: jnp.broadcast_to(jnp.asarray(zero, part.dtype), part.shape), x, identity
    )

    def lap(k, before):
        reached = k < index
        new = combine(
            before, jax.tree.map(lambda part, own: part[k].astype(own.dtype), everything, x)
        )
        return jax.tree.map(lambda a, b: jnp.where(reached, a, b), new, before)

    return lax.fori_loop(0, count, lap, start)


def unit_rows(value_rows_drawn):
    return value_rows_drawn / jnp.sqrt(
        jnp.sum(value_rows_drawn * value_rows_drawn, axis=-1, keepdims=True) + 1e-06
    )


def stretch_terms(query_rows_drawn, key_rows_drawn, value_rows_drawn, strength, log_decay):
    span_len = query_rows_drawn.shape[1]
    cumul = jnp.cumsum(log_decay, axis=-1)
    later = jnp.arange(span_len)[:, None]
    earlier = jnp.arange(span_len)[None, :]
    strict = (later > earlier)[None]
    within = (later >= earlier)[None]
    spread = cumul[:, :, None] - cumul[:, None, :]
    ratio_within = jnp.where(within, jnp.exp(jnp.where(within, spread, 0.0)), 0.0)
    intersection = jnp.einsum("hcd,hed->hce", key_rows_drawn, key_rows_drawn, precision=precise)
    lower = jnp.where(strict, strength[:, :, None] * ratio_within * intersection, 0.0)
    identity = jnp.eye(span_len, dtype=jnp.float32)[None]
    power = -lower
    inverse = identity + power
    reach = 2
    while reach < span_len:
        power = jnp.einsum("hij,hjk->hik", power, power, precision=precise)
        inverse = jnp.einsum("hij,hjk->hik", inverse, identity + power, precision=precise)
        reach = reach * 2
    transform = inverse * strength[:, None, :]
    growth = jnp.exp(cumul)
    mixed_keys = jnp.einsum(
        "hij,hjd->hid", transform, growth[:, :, None] * key_rows_drawn, precision=precise
    )
    mixed_values = jnp.einsum("hij,hjd->hid", transform, value_rows_drawn, precision=precise)
    attend = (
        jnp.einsum("hcd,hed->hce", query_rows_drawn, key_rows_drawn, precision=precise)
        * ratio_within
    )
    reduced = growth[:, :, None] * query_rows_drawn - jnp.einsum(
        "hij,hjd->hid", attend, mixed_keys, precision=precise
    )
    local_out = jnp.einsum("hij,hjd->hid", attend, mixed_values, precision=precise)
    carried_keys = jnp.exp(cumul[:, -1:] - cumul)[:, :, None] * key_rows_drawn
    final_decay = jnp.exp(cumul[:, -1])
    key_width = key_rows_drawn.shape[2]
    transition = final_decay[:, None, None] * jnp.eye(key_width, dtype=jnp.float32)[
        None
    ] - jnp.einsum("hcd,hce->hde", carried_keys, mixed_keys, precision=precise)
    injected = jnp.einsum("hcd,hce->hde", carried_keys, mixed_values, precision=precise)
    return (reduced, local_out, transition, injected)


def compose_maps(earlier, later):
    return (
        jnp.einsum("hij,hjk->hik", later[0], earlier[0], precision=precise),
        jnp.einsum("hij,hjk->hik", later[0], earlier[1], precision=precise) + later[1],
    )


def body(
    residual,
    sliding_query_heads,
    sliding_key_heads,
    sliding_value_heads,
    output_weight,
    norm_gain,
    query_weight,
    key_weight,
    value_weight,
    write_strength,
    log_decay,
):
    shard_rows = sliding_query_heads.shape[0]
    seq_count = lax.axis_size("seq")
    kv_local = sliding_key_heads.shape[1] // HEAD_WIDTH
    share_fraction = QUERY_HEADS // KEY_VALUE_HEADS
    behind = min((WINDOW_KEYS + shard_rows - 2) // shard_rows, seq_count - 1)
    earlier_keys = []
    earlier_values = []
    for distance in range(behind, 0, -1):
        moved_keys, moved_values = shifted(
            (sliding_key_heads, sliding_value_heads), "seq", distance
        )
        earlier_keys.append(moved_keys)
        earlier_values.append(moved_values)
    key_rows = jnp.concatenate(earlier_keys + [sliding_key_heads], axis=0)
    value_rows = jnp.concatenate(earlier_values + [sliding_value_heads], axis=0)
    first_row = lax.axis_index("seq") * shard_rows
    query_pos = first_row + jnp.arange(shard_rows)
    key_pos = first_row - behind * shard_rows + jnp.arange((behind + 1) * shard_rows)
    valid = (
        (key_pos[None, :] <= query_pos[:, None])
        & (key_pos[None, :] > query_pos[:, None] - WINDOW_KEYS)
        & (key_pos[None, :] >= 0)
    )
    grouped = sliding_query_heads.reshape(
        shard_rows, kv_local, share_fraction, HEAD_WIDTH
    ).transpose(2, 1, 0, 3)
    key_heads = key_rows.reshape(-1, kv_local, HEAD_WIDTH)
    value_heads = value_rows.reshape(-1, kv_local, HEAD_WIDTH)

    def one_head(query_rows_drawn):
        scores = jnp.einsum(
            "gqd,kgd->gqk", query_rows_drawn, key_heads, preferred_element_type=jnp.float32
        ) / math.sqrt(HEAD_WIDTH)
        scores = jnp.where(valid[None], scores, -1e30)
        highest = jnp.max(scores, axis=-1, keepdims=True)
        weights = jnp.exp(scores - highest)
        weights = (weights / jnp.sum(weights, axis=-1, keepdims=True)).astype(jnp.bfloat16)
        return jnp.einsum(
            "gqk,kgd->gqd", weights, value_heads, preferred_element_type=jnp.float32
        ).astype(jnp.bfloat16)

    attended = lax.map(one_head, grouped).transpose(2, 1, 0, 3).reshape(shard_rows, -1)
    summed = lax.psum_scatter(
        jnp.dot(attended, output_weight, preferred_element_type=jnp.float32).astype(jnp.bfloat16),
        "head",
        scatter_dimension=0,
        tiled=True,
    ).astype(jnp.float32)
    mixed_stream = (residual.astype(jnp.float32) + summed).astype(jnp.bfloat16)
    stream = mixed_stream.astype(jnp.float32)
    normed = (
        stream * lax.rsqrt(jnp.mean(stream * stream, axis=-1, keepdims=True) + 1e-06) * norm_gain
    ).astype(jnp.bfloat16)
    piece = lax.all_gather(normed, "head", axis=0, tiled=True)
    lifted = jnp.concatenate(
        [
            jnp.dot(piece, query_weight, preferred_element_type=jnp.float32),
            jnp.dot(piece, key_weight, preferred_element_type=jnp.float32),
            jnp.dot(piece, value_weight, preferred_element_type=jnp.float32),
        ],
        axis=1,
    )
    qk_width = query_weight.shape[1]
    heads_local = value_weight.shape[1] // HEAD_WIDTH
    group_size = DELTA_VALUE_HEADS // HK
    query_rows_drawn = unit_rows(lifted[:, :qk_width].reshape(shard_rows, -1, HEAD_WIDTH))
    key_rows_drawn = unit_rows(
        lifted[:, qk_width : 2 * qk_width].reshape(shard_rows, -1, HEAD_WIDTH)
    )
    value_rows_drawn = lifted[:, 2 * qk_width :].reshape(shard_rows, heads_local, HEAD_WIDTH)
    query_rows_drawn = jnp.repeat(query_rows_drawn.transpose(1, 0, 2), group_size, axis=0)
    key_rows_drawn = jnp.repeat(key_rows_drawn.transpose(1, 0, 2), group_size, axis=0)
    value_rows_drawn = value_rows_drawn.transpose(1, 0, 2)
    blocks = shard_rows // CH

    def split_blocks(array):
        return array.reshape(heads_local, blocks, CH, HEAD_WIDTH).transpose(1, 0, 2, 3)

    block_inputs = (
        split_blocks(query_rows_drawn),
        split_blocks(key_rows_drawn),
        split_blocks(value_rows_drawn),
        write_strength.reshape(heads_local, blocks, CH).transpose(1, 0, 2),
        log_decay.reshape(heads_local, blocks, CH).transpose(1, 0, 2),
    )
    unit_map = jnp.broadcast_to(
        jnp.eye(HEAD_WIDTH, dtype=jnp.float32)[None], (heads_local, HEAD_WIDTH, HEAD_WIDTH)
    )
    empty_state = jnp.zeros((heads_local, HEAD_WIDTH, HEAD_WIDTH), jnp.float32)

    def advance(carry, block):
        through, gathered = carry
        reduced, local_out, transition, injected = stretch_terms(*block)
        twisted = jnp.einsum("hcd,hde->hce", reduced, through, precision=precise)
        readout = jnp.einsum("hcd,hde->hce", reduced, gathered, precision=precise) + local_out
        gathered = jnp.einsum("hde,hef->hdf", transition, gathered, precision=precise) + injected
        through = jnp.einsum("hde,hef->hdf", transition, through, precision=precise)
        return ((through, gathered), (twisted, readout))

    (through, gathered), (twisted_all, local_readouts) = lax.scan(
        advance, (unit_map, empty_state), block_inputs
    )
    prefix = carried_in((through, gathered), "seq", compose_maps, (unit_map, empty_state))
    incoming = prefix[1]
    readouts = local_readouts + jnp.einsum(
        "nhcd,hde->nhce", twisted_all, incoming, precision=precise
    )
    delta_output = (
        readouts.transpose(1, 0, 2, 3)
        .reshape(heads_local, shard_rows, HEAD_WIDTH)
        .transpose(1, 0, 2)
        .reshape(shard_rows, heads_local * HEAD_WIDTH)
    )
    return (mixed_stream, delta_output.astype(jnp.bfloat16))


def solution(mesh):
    in_specs = (
        P(("seq", "head"), None),
        P("seq", "head"),
        P("seq", "head"),
        P("seq", "head"),
        P("head", None),
        P(),
        P(None, "head"),
        P(None, "head"),
        P(None, "head"),
        P("head", "seq"),
        P("head", "seq"),
    )
    out_specs = (P(("seq", "head"), None), P("seq", "head"))
    return jax.shard_map(body, mesh=mesh, in_specs=in_specs, out_specs=out_specs, check_vma=False)
```

profile of v0, /device:TPU:1, one launch (start us, length us, event | category | flops | bytes accessed | tf_op | source)
XLA Modules:
  0.0 478.0 jit_solution(14976653959303377444)
XLA Ops:
  7.2 4.1 collective-permute-start
  11.3 4.0 collective-permute-start.1
  15.3 4.6 collective-permute-start.2
  20.0 2.6 collective-permute-start.3
  22.6 4.5 collective-permute-start.4
  28.5 3.0 collective-permute-start.5
  31.5 2.3 collective-permute-start.6
  33.8 3.0 collective-permute-start.7
  36.9 1.3 collective-permute-start.8
  38.3 1.3 collective-permute-start.9
  39.6 3.2 collective-permute-start.10
  42.9 2.2 collective-permute-start.11
  45.1 2.0 collective-permute-start.12
  47.2 4.8 collective-permute-start.13
  52.0 1.7 collective-permute-start.14
  53.7 2.1 collective-permute-start.15
  57.0 1.3 collective-permute-done.15
  59.4 35.1 %while.42 = (s32[]{:T(128)}, bf16[4,1,512,128]{2,3,0,1:T(8,128)(2,1)S(1)}, bf16[4,1,512,128]{2,3,0,1:T(8,128)(2,1)S(1)}, bf16[4608,1,128]{2,0,1:T(8,128)(2,1)}, ...) while((s32[]{:T(128)}, ...), condition=%wide.region_3.4_spmd.clone, body=%wide.region_0.3_spmd.clone.sunk | while | flops 1236335616 | bytes 36215944 | solution.py:155
  59.4 4.9 %fusion.193 = (f32[512]{0:T(512)S(1)}, f32[512,4608]{1,0:T(8,128)S(1)}) fusion(bf16[4608,1,128]{2,0,1:T(8,128)(2,1)} %get-tuple-element.552, bf16[4,1,512,128]{2,3,0,1:T(8,128)(2,1)S(1)} %get-tuple-element.551, s32[]{:T(128)} %get-tuple-element.539, pred[4608]{0:T(1024)(128)(4,1)S(1)} %get-tuple-element.557, s32[512]{0:T(512)S(1)} %get-tuple-element.555, ...), kind=kOutput, calls=%fused_computation.138.clone.1 | convolution fusion | flops 620494336 | bytes 10779652 | tf_op jit(solution)/shard_map/while/body/eval_jaxpr/gqd,kgd->gqk/dot_general | solution.py:144
  64.4 1.4 fusion.194
  65.8 2.3 fusion.195
  68.2 4.9 %fusion.193 = (f32[512]{0:T(512)S(1)}, f32[512,4608]{1,0:T(8,128)S(1)}) fusion(bf16[4608,1,128]{2,0,1:T(8,128)(2,1)} %get-tuple-element.552, bf16[4,1,512,128]{2,3,0,1:T(8,128)(2,1)S(1)} %get-tuple-element.551, s32[]{:T(128)} %get-tuple-element.539, pred[4608]{0:T(1024)(128)(4,1)S(1)} %get-tuple-element.557, s32[512]{0:T(512)S(1)} %get-tuple-element.555, ...), kind=kOutput, calls=%fused_computation.138.clone.1 | convolution fusion | flops 620494336 | bytes 10779652 | tf_op jit(solution)/shard_map/while/body/eval_jaxpr/gqd,kgd->gqk/dot_general | solution.py:144
  73.1 1.4 fusion.194
  74.6 2.3 fusion.195
  77.0 4.9 %fusion.193 = (f32[512]{0:T(512)S(1)}, f32[512,4608]{1,0:T(8,128)S(1)}) fusion(bf16[4608,1,128]{2,0,1:T(8,128)(2,1)} %get-tuple-element.552, bf16[4,1,512,128]{2,3,0,1:T(8,128)(2,1)S(1)} %get-tuple-element.551, s32[]{:T(128)} %get-tuple-element.539, pred[4608]{0:T(1024)(128)(4,1)S(1)} %get-tuple-element.557, s32[512]{0:T(512)S(1)} %get-tuple-element.555, ...), kind=kOutput, calls=%fused_computation.138.clone.1 | convolution fusion | flops 620494336 | bytes 10779652 | tf_op jit(solution)/shard_map/while/body/eval_jaxpr/gqd,kgd->gqk/dot_general | solution.py:144
  81.9 1.4 fusion.194
  83.3 2.3 fusion.195
  85.8 4.9 %fusion.193 = (f32[512]{0:T(512)S(1)}, f32[512,4608]{1,0:T(8,128)S(1)}) fusion(bf16[4608,1,128]{2,0,1:T(8,128)(2,1)} %get-tuple-element.552, bf16[4,1,512,128]{2,3,0,1:T(8,128)(2,1)S(1)} %get-tuple-element.551, s32[]{:T(128)} %get-tuple-element.539, pred[4608]{0:T(1024)(128)(4,1)S(1)} %get-tuple-element.557, s32[512]{0:T(512)S(1)} %get-tuple-element.555, ...), kind=kOutput, calls=%fused_computation.138.clone.1 | convolution fusion | flops 620494336 | bytes 10779652 | tf_op jit(solution)/shard_map/while/body/eval_jaxpr/gqd,kgd->gqk/dot_general | solution.py:144
  90.7 1.4 fusion.194
  92.1 2.3 fusion.195
  94.6 6.5 %convolution_convert_fusion = bf16[512,4096]{1,0:T(8,128)(2,1)} fusion(bf16[512,512]{0,1:T(8,128)(2,1)S(1)} %bitcast.242, bf16[512,4096]{1,0:T(8,128)(2,1)} %param.21), kind=kOutput, calls=%fused_computation.95 | convolution fusion | flops 2149580800 | bytes 8912896 | tf_op jit(solution)/shard_map/dot_general | solution.py:157
  101.2 58.0 %reduce-scatter.2.cloned.1.call-done = bf16[64,4096]{1,0:T(8,128)(2,1)} async-done(((bf16[512,4096]{1,0:T(8,128)(2,1)}), bf16[64,4096]{1,0:T(8,128)(2,1)}) %reduce-scatter.2.cloned.1.call-update) | async-done | bytes 524304 | tf_op jit(solution)/shard_map/reduce_scatter | solution.py:156
  159.2 1.3 fusion.76
  162.8 53.1 %all-gather.6.cloned.1.call-done = bf16[512,4096]{1,0:T(8,128)(2,1)} async-done(((bf16[64,4096]{1,0:T(8,128)(2,1)}), bf16[512,4096]{1,0:T(8,128)(2,1)}) %all-gather.6.cloned.1.call-update) | async-done | bytes 4194320 | tf_op jit(solution)/shard_map/all_gather | solution.py:167
  215.9 3.7 multiply_reduce_fusion
  219.6 1.4 multiply_reduce_fusion.1
  221.8 2.4 fusion.88
  224.2 1.3 copy.29
  227.0 96.2 %while.43 = (s32[]{:T(128)}, f32[4,128,128]{2,1,0:T(8,128)S(1)}, f32[4,128,128]{2,1,0:T(8,128)S(1)}, f32[8,4,64,128]{3,2,0,1:T(8,128)}, f32[8,4,64,128]{3,2,0,1:...) while((s32[]{:T(128)}, f32[4,128,128]{2,1,0:T(8,128)S(1)}, ...), condition=%wide.region_10.11_spmd.clone, body=%wide.region_8.10_spmd.clone.sunk | while | flops 680361984 | bytes 8550644 | solution.py:213
  324.7 49.5 %all-gather.8.cloned.1.call-done = bf16[128,128,128]{2,1,0:T(8,128)(2,1)} async-done(((bf16[4,128,128]{2,1,0:T(8,128)(2,1)}), bf16[128,128,128]{2,1,0:T(8,128)(2,1)}) %all-gather.8.cloned.1.call-update) | async-done | bytes 4194320 | tf_op jit(solution)/shard_map/all_gather | solution.py:29
  374.2 53.0 %all-gather.10.cloned.1.call-done = bf16[128,128,128]{2,1,0:T(8,128)(2,1)} async-done(((bf16[4,128,128]{2,1,0:T(8,128)(2,1)}), bf16[128,128,128]{2,1,0:T(8,128)(2,1)}) %all-gather.10.cloned.1.call-update) | async-done | bytes 4194320 | tf_op jit(solution)/shard_map/all_gather | solution.py:29
  427.2 42.4 %while.44 = (s32[]{:T(128)}, f32[4,128,128]{2,1,0:T(8,128)S(1)}, s32[]{:T(128)}, bf16[32,4,128,128]{3,2,1,0:T(8,128)(2,1)}, bf16[32,4,128,128]{3,2,1,0:T(8,128)(2,1)}, /*index=5*/s32[]{:T(128)}, s32[]{:T(128)}) while((s32[]{:T(128)}, f32[4,128,128]{2,1,0:T(8,128)S(1)}, s32[]{:T(128)}, bf16[32,4,128,128]{3,2,1,0:T(8,128)(2,1)}, ...), condition=%wide.region_12.13_spmd.clone, body=%wide.region_11.12_spmd.clone.sunk | while | flops 100990976 | bytes 1575519 | solution.py:42
  427.2 1.3 fusion.256
  428.6 1.3 fusion.256
  429.9 1.3 fusion.256
  431.3 1.3 fusion.256
  432.6 1.3 fusion.256
  433.9 1.3 fusion.256
  435.2 1.3 fusion.256
  437.9 1.3 fusion.256
  439.2 1.3 fusion.256
  440.5 1.3 fusion.256
  443.2 1.3 fusion.256
  444.5 1.3 fusion.256
  445.8 1.3 fusion.256
  448.4 1.3 fusion.256
  449.8 1.3 fusion.256
  451.1 1.3 fusion.256
  452.4 1.3 fusion.256
  453.7 1.3 fusion.256
  455.1 1.3 fusion.256
  456.4 1.3 fusion.256
  457.7 1.3 fusion.256
  459.0 1.3 fusion.256
  (402 shorter events, 120.0 us)
Async XLA Ops:
  7.2 208.8 %copy-start = (bf16[4096,128]{1,0:T(8,128)(2,1)S(1)}, bf16[4096,128]{1,0:T(8,128)(2,1)}, u32[]{:S(2)}) copy-start(bf16[4096,128]{1,0:T(8,128)(2,1)} %param.23) | copy-start | bytes 3145732
  7.2 24.3 %copy-start.5 = (bf16[512,128]{1,0:T(8,128)(2,1)S(1)}, bf16[512,128]{1,0:T(8,128)(2,1)}, u32[]{:S(2)}) copy-start(bf16[512,128]{1,0:T(8,128)(2,1)} %param.19) | copy-start | bytes 393220
  7.2 29.7 %copy-start.6 = (bf16[512,128]{1,0:T(8,128)(2,1)S(1)}, bf16[512,128]{1,0:T(8,128)(2,1)}, u32[]{:S(2)}) copy-start(bf16[512,128]{1,0:T(8,128)(2,1)} %param.20) | copy-start | bytes 393220
  7.2 152.0 %reduce-scatter.2.cloned.1.call-start = ((), (), s32[]{:S(2)}) async-start(), calls=%async_computation.1 | async-start | bytes 4718592 | tf_op jit(solution)/shard_map/reduce_scatter | solution.py:156
  7.2 21.2 %collective-permute-start = (bf16[512,128]{1,0:T(8,128)(2,1)}, bf16[512,128]{1,0:T(8,128)(2,1)S(1)}, u32[]{:S(2)}, u32[]{:S(2)}) collective-permute-start(bf16[512,128]{1,0:T(8,128)(2,1)} %param.19), channel_id=1, source_target_pairs={{0,64},{8,72},{16,80},{24,88},{32,96},{40,104},{48,112},{56,120},{... | collective-permute-start | bytes 393224 | tf_op jit(solution)/shard_map/ppermute | solution.py:23
  11.3 20.1 %collective-permute-start.1 = (bf16[512,128]{1,0:T(8,128)(2,1)}, bf16[512,128]{1,0:T(8,128)(2,1)S(1)}, u32[]{:S(2)}, u32[]{:S(2)}) collective-permute-start(bf16[512,128]{1,0:T(8,128)(2,1)} %param.19), channel_id=1, source_target_pairs={{0,56},{8,64},{16,72},{24,80},{32,88},{40,96},{48,104},{56,112},{6... | collective-permute-start | bytes 393224 | tf_op jit(solution)/shard_map/ppermute | solution.py:23
  15.3 18.5 %collective-permute-start.2 = (bf16[512,128]{1,0:T(8,128)(2,1)}, bf16[512,128]{1,0:T(8,128)(2,1)S(1)}, u32[]{:S(2)}, u32[]{:S(2)}) collective-permute-start(bf16[512,128]{1,0:T(8,128)(2,1)} %param.19), channel_id=1, source_target_pairs={{0,48},{8,56},{16,64},{24,72},{32,80},{40,88},{48,96},{56,104},{64... | collective-permute-start | bytes 393224 | tf_op jit(solution)/shard_map/ppermute | solution.py:23
  20.0 16.9 %collective-permute-start.3 = (bf16[512,128]{1,0:T(8,128)(2,1)}, bf16[512,128]{1,0:T(8,128)(2,1)S(1)}, u32[]{:S(2)}, u32[]{:S(2)}) collective-permute-start(bf16[512,128]{1,0:T(8,128)(2,1)} %param.19), channel_id=1, source_target_pairs={{0,40},{8,48},{16,56},{24,64},{32,72},{40,80},{48,88},{56,96},{64,... | collective-permute-start | bytes 393224 | tf_op jit(solution)/shard_map/ppermute | solution.py:23
  22.6 15.7 %collective-permute-start.4 = (bf16[512,128]{1,0:T(8,128)(2,1)}, bf16[512,128]{1,0:T(8,128)(2,1)S(1)}, u32[]{:S(2)}, u32[]{:S(2)}) collective-permute-start(bf16[512,128]{1,0:T(8,128)(2,1)} %param.19), channel_id=1, source_target_pairs={{0,32},{8,40},{16,48},{24,56},{32,64},{40,72},{48,80},{56,88},{64,... | collective-permute-start | bytes 393224 | tf_op jit(solution)/shard_map/ppermute | solution.py:23
  28.5 11.2 %collective-permute-start.5 = (bf16[512,128]{1,0:T(8,128)(2,1)}, bf16[512,128]{1,0:T(8,128)(2,1)S(1)}, u32[]{:S(2)}, u32[]{:S(2)}) collective-permute-start(bf16[512,128]{1,0:T(8,128)(2,1)} %param.19), channel_id=1, source_target_pairs={{0,24},{8,32},{16,40},{24,48},{32,56},{40,64},{48,72},{56,80},{64,... | collective-permute-start | bytes 393224 | tf_op jit(solution)/shard_map/ppermute | solution.py:23
  31.5 11.4 %collective-permute-start.6 = (bf16[512,128]{1,0:T(8,128)(2,1)S(1)}, bf16[512,128]{1,0:T(8,128)(2,1)S(1)}, u32[]{:S(2)}, u32[]{:S(2)}) collective-permute-start(bf16[512,128]{1,0:T(8,128)(2,1)S(1)} %copy-done.5), channel_id=1, source_target_pairs={{0,16},{8,24},{16,32},{24,40},{32,48},{40,56},{48,64},{56,72},{64,... | collective-permute-start | bytes 393224 | tf_op jit(solution)/shard_map/ppermute | solution.py:23
  33.8 11.2 %collective-permute-start.7 = (bf16[512,128]{1,0:T(8,128)(2,1)S(1)}, bf16[512,128]{1,0:T(8,128)(2,1)S(1)}, u32[]{:S(2)}, u32[]{:S(2)}) collective-permute-start(bf16[512,128]{1,0:T(8,128)(2,1)S(1)} %copy-done.5), channel_id=1, source_target_pairs={{0,8},{8,16},{16,24},{24,32},{32,40},{40,48},{48,56},{56,64},{64,7... | collective-permute-start | bytes 393224 | tf_op jit(solution)/shard_map/ppermute | solution.py:23
  36.9 10.3 %collective-permute-start.8 = (bf16[512,128]{1,0:T(8,128)(2,1)S(1)}, bf16[512,128]{1,0:T(8,128)(2,1)S(1)}, u32[]{:S(2)}, u32[]{:S(2)}) collective-permute-start(bf16[512,128]{1,0:T(8,128)(2,1)S(1)} %copy-done.6), channel_id=1, source_target_pairs={{0,64},{8,72},{16,80},{24,88},{32,96},{40,104},{48,112},{56,120},{... | collective-permute-start | bytes 393224 | tf_op jit(solution)/shard_map/ppermute | solution.py:23
  38.3 13.7 %collective-permute-start.9 = (bf16[512,128]{1,0:T(8,128)(2,1)S(1)}, bf16[512,128]{1,0:T(8,128)(2,1)S(1)}, u32[]{:S(2)}, u32[]{:S(2)}) collective-permute-start(bf16[512,128]{1,0:T(8,128)(2,1)S(1)} %copy-done.6), channel_id=1, source_target_pairs={{0,56},{8,64},{16,72},{24,80},{32,88},{40,96},{48,104},{56,112},{6... | collective-permute-start | bytes 393224 | tf_op jit(solution)/shard_map/ppermute | solution.py:23
  39.6 14.1 %collective-permute-start.10 = (bf16[512,128]{1,0:T(8,128)(2,1)S(1)}, bf16[512,128]{1,0:T(8,128)(2,1)S(1)}, u32[]{:S(2)}, u32[]{:S(2)}) collective-permute-start(bf16[512,128]{1,0:T(8,128)(2,1)S(1)} %copy-done.6), channel_id=1, source_target_pairs={{0,48},{8,56},{16,64},{24,72},{32,80},{40,88},{48,96},{56,104},{64... | collective-permute-start | bytes 393224 | tf_op jit(solution)/shard_map/ppermute | solution.py:23
  42.9 13.0 %collective-permute-start.11 = (bf16[512,128]{1,0:T(8,128)(2,1)S(1)}, bf16[512,128]{1,0:T(8,128)(2,1)S(1)}, u32[]{:S(2)}, u32[]{:S(2)}) collective-permute-start(bf16[512,128]{1,0:T(8,128)(2,1)S(1)} %copy-done.6), channel_id=1, source_target_pairs={{0,40},{8,48},{16,56},{24,64},{32,72},{40,80},{48,88},{56,96},{64,... | collective-permute-start | bytes 393224 | tf_op jit(solution)/shard_map/ppermute | solution.py:23
  45.1 10.8 %collective-permute-start.12 = (bf16[512,128]{1,0:T(8,128)(2,1)S(1)}, bf16[512,128]{1,0:T(8,128)(2,1)S(1)}, u32[]{:S(2)}, u32[]{:S(2)}) collective-permute-start(bf16[512,128]{1,0:T(8,128)(2,1)S(1)} %copy-done.6), channel_id=1, source_target_pairs={{0,32},{8,40},{16,48},{24,56},{32,64},{40,72},{48,80},{56,88},{64,... | collective-permute-start | bytes 393224 | tf_op jit(solution)/shard_map/ppermute | solution.py:23
  47.2 11.2 %copy-start.8 = (bf16[4608,128]{1,0:T(8,128)(2,1)}, bf16[4608,128]{1,0:T(8,128)(2,1)S(1)}, u32[]{:S(2)}) copy-start(bf16[4608,128]{1,0:T(8,128)(2,1)S(1)} %constant_dynamic-update-slice_fusion.1) | copy-start | bytes 3538948
  47.2 8.7 %collective-permute-start.13 = (bf16[512,128]{1,0:T(8,128)(2,1)S(1)}, bf16[512,128]{1,0:T(8,128)(2,1)S(1)}, u32[]{:S(2)}, u32[]{:S(2)}) collective-permute-start(bf16[512,128]{1,0:T(8,128)(2,1)S(1)} %copy-done.6), channel_id=1, source_target_pairs={{0,24},{8,32},{16,40},{24,48},{32,56},{40,64},{48,72},{56,80},{64,... | collective-permute-start | bytes 393224 | tf_op jit(solution)/shard_map/ppermute | solution.py:23
  52.0 5.0 %collective-permute-start.14 = (bf16[512,128]{1,0:T(8,128)(2,1)S(1)}, bf16[512,128]{1,0:T(8,128)(2,1)S(1)}, u32[]{:S(2)}, u32[]{:S(2)}) collective-permute-start(bf16[512,128]{1,0:T(8,128)(2,1)S(1)} %copy-done.6), channel_id=1, source_target_pairs={{0,16},{8,24},{16,32},{24,40},{32,48},{40,56},{48,64},{56,72},{64,... | collective-permute-start | bytes 393224 | tf_op jit(solution)/shard_map/ppermute | solution.py:23
  53.7 4.6 collective-permute-start.15
  58.4 1.0 copy-start.9
  64.3 1.4 copy-start.10
  73.1 1.4 copy-start.10
  81.9 1.4 copy-start.10
  90.7 1.4 copy-start.10
  101.1 58.1 %copy-start.4 = (bf16[64,4096]{1,0:T(8,128)(2,1)S(1)}, bf16[64,4096]{1,0:T(8,128)(2,1)}, u32[]{:S(2)}) copy-start(bf16[64,4096]{1,0:T(8,128)(2,1)} %param.17) | copy-start | bytes 1572868
  101.1 60.2 %copy-start.7 = (f32[4096]{0:T(1024)S(1)}, f32[4096]{0:T(1024)}, u32[]{:S(2)}) copy-start(f32[4096]{0:T(1024)} %param.22) | copy-start | bytes 49156
  101.2 114.8 %all-gather.6.cloned.1.call-start = ((), (), s32[]{:S(2)}) async-start(), calls=%async_computation.2 | async-start | bytes 4718592 | tf_op jit(solution)/shard_map/all_gather | solution.py:167
  160.5 0.8 copy-start.1
  160.6 2.1 copy-start.11
  160.6 2.1 copy-start.12
  162.3 211.9 %all-gather.8.cloned.1.call-start = ((), (), s32[]{:S(2)}) async-start(), calls=%async_computation.3 | async-start | bytes 4325376 | tf_op jit(solution)/shard_map/all_gather | solution.py:29
  162.8 56.8 %copy-start.15 = (bf16[4096,128]{1,0:T(8,128)(2,1)S(1)}, bf16[4096,128]{1,0:T(8,128)(2,1)}, u32[]{:S(2)}) copy-start(bf16[4096,128]{1,0:T(8,128)(2,1)} %param.24) | copy-start | bytes 3145732
  215.9 3.7 copy-start.14
  219.6 2.2 copy-start.13
  323.2 146.3 %copy-start.3 = (f32[8,4,64,128]{3,2,0,1:T(8,128)S(1)}, f32[8,4,64,128]{3,2,0,1:T(8,128)}, u32[]{:S(2)}) copy-start(f32[8,4,64,128]{3,2,0,1:T(8,128)} %get-tuple-element.184) | copy-start | bytes 3145732
  324.0 103.2 %all-gather.10.cloned.1.call-start = ((), (), s32[]{:S(2)}) async-start(), calls=%async_computation.4 | async-start | bytes 4325376 | tf_op jit(solution)/shard_map/all_gather | solution.py:29
  427.2 42.4 %copy-start.2 = (f32[8,4,64,128]{3,2,0,1:T(8,128)S(1)}, f32[8,4,64,128]{3,2,0,1:T(8,128)}, u32[]{:S(2)}) copy-start(f32[8,4,64,128]{3,2,0,1:T(8,128)} %get-tuple-element.188) | copy-start | bytes 3145732
Sparse Core Ops, SparseCore 0:
  101.3 57.8 reduce-scatter.1
  162.5 53.3 all-gather.5
  324.1 50.0 all-gather.7
  376.6 50.5 all-gather.9
where the time goes:
time: 480 us; the launch traced here: 478 us
  waiting for transfers between devices  216 us (45%)
  matrix products  174 us (36%)
  starting transfers between devices  47.1 us (10%)
  between operations  14.5 us (3%)
  other arithmetic  12.4 us (3%)
  local copies, waits for them, and re-layouts  10.7 us (2%)
    all_gather x2, waiting for transfers between devices, carried_in(): lax.all_gather(part.astype(kind), axis)  102 us
    reduce_scatter x1, waiting for transfers between devices, body(): lax.psum_scatter(jnp.dot(attended, output_weight, preferred_element_type=...  58 us
    all_gather x1, waiting for transfers between devices, body(): piece = lax.all_gather(normed, 'head', axis=0, tiled=True)  53.1 us
    ppermute x16, starting transfers between devices, shifted(): return lax.ppermute(x, axis, pairs)  46.7 us
    dot_general x32, matrix products, compose_maps(): jnp.einsum('hij,hjk->hik', later[0], earlier[1], precision=precise)  40.6 us
    dot_general x4, matrix products, one_head(): jnp.einsum('gqd,kgd->gqk', query_rows_drawn, key_heads, preferred_element...  19.6 us
    dot_general x40, matrix products, stretch_terms(): jnp.einsum('hij,hjk->hik', inverse, identity + power, precision=precise)  10.3 us
    dot_general x40, matrix products, stretch_terms(): power = jnp.einsum('hij,hjk->hik', power, power, precision=precise)  10.2 us
  transfers between devices with their start and end apart: 20, of which 6 were waited for; matrix products, arithmetic and copies ran while one was open for 1% of the time, Pallas kernels for 0%

commit v1 on v0

v1 whole, which is shorter than its diff:
```python
import functools
import math

import jax
import jax.numpy as jnp
from jax import lax
from jax.experimental import pallas as pl
from jax.experimental.pallas import tpu as pltpu
from jax.sharding import Mesh
from jax.sharding import PartitionSpec as P

bf = jnp.bfloat16
f32 = jnp.float32
HW = 128
G = 4
WINDOW = 4096
TOK = 512
NEG = -1e30
SCALE = math.log2(math.e) / math.sqrt(HW)
RT = 128
CK = 512
C = 64
W4 = G * C
SEQ = ("x", "y", "c")


def attention_kernel(q0, low_ref, q_ref, own_ref, d2_ref, d4_ref, d6_ref, d8_ref, odd_ref, w_ref, out_ref,
                     keys, values, scores, top, acc, att):
    rows=q_ref.shape[0]
    tiles=rows//RT
    srcs={0:own_ref,2:d2_ref,4:d4_ref,6:d6_ref,8:d8_ref}
    low=low_ref[0]
    lane=lax.broadcasted_iota(jnp.int32,(512,HW),1)
    for d in range(9):
        at=(8-d)*512
        src=srcs[d] if d in srcs else odd_ref.at[(d-1)//2]
        keys[at:at+512,:HW]=src[:,:HW]
        values[at:at+512,:HW]=src[:,HW:]
        gone=jnp.where(at<low,NEG,0.0)
        keys[at:at+512,HW:]=jnp.where(lane==0,gone,0.0).astype(jnp.bfloat16)
        values[at:at+512,HW:]=jnp.ones((512,HW),jnp.bfloat16)
    r=lax.broadcasted_iota(jnp.int32,(G*RT,HW),0)%RT
    c=lax.broadcasted_iota(jnp.int32,(G*RT,HW),1)
    oldest=c>r
    unit=jnp.where(c==0,1.0,0.0).astype(jnp.bfloat16)

    def queries(t):
        q=q_ref[t*RT:(t+1)*RT,:]
        q=jnp.concatenate([q[:,h*HW:(h+1)*HW] for h in range(G)],axis=0)
        return jnp.concatenate([q,unit],axis=1)

    def dot_t(a,b):
        return lax.dot_general(a,b,(((1,),(1,)),((),())),preferred_element_type=jnp.float32)

    def score(t,j,first):
        base=q0+t*RT
        at=base+j*CK if isinstance(j,int) else pl.multiple_of(base+j*CK,RT)
        s=dot_t(queries(t),keys[pl.ds(at,CK),:])
        if first:
            last=dot_t(queries(t),keys[pl.ds(base+4096,RT),:])
            s=jnp.concatenate([jnp.where(oldest,s[:,:HW],last),s[:,HW:]],axis=1)
        scores[t%2,:,pl.ds(j*CK if isinstance(j,int) else pl.multiple_of(j*CK,CK),CK)]=s
        m=functools.reduce(jnp.maximum,[s[:,i*HW:(i+1)*HW] for i in range(CK//HW)])
        if first: top[t%2]=m
        else: top[t%2]=jnp.maximum(top[t%2],m)

    def weigh(t,j,first,m):
        base=q0+t*RT
        at=base+j*CK if isinstance(j,int) else pl.multiple_of(base+j*CK,RT)
        s=scores[t%2,:,pl.ds(j*CK if isinstance(j,int) else pl.multiple_of(j*CK,CK),CK)]
        p=jnp.concatenate([jnp.exp2((s[:,i*HW:(i+1)*HW]-m)*SCALE) for i in range(CK//HW)],axis=1).astype(jnp.bfloat16)
        if first:
            pa=p[:,:HW]
            zero=jnp.zeros_like(pa)
            new=jnp.where(oldest,zero,pa)
            old=jnp.where(oldest,pa,zero)
            p=jnp.concatenate([old,p[:,HW:],new],axis=1)
            v=jnp.concatenate([values[pl.ds(at,CK),:],values[pl.ds(base+4096,RT),:]],axis=0)
            acc[...]=jnp.dot(p,v,preferred_element_type=jnp.float32)
        else:
            acc[...]+=jnp.dot(p,values[pl.ds(at,CK),:],preferred_element_type=jnp.float32)


    steps=4096//CK
    score(0,0,True)
    def pre(j,_):
        score(0,j,False)
        return _
    lax.fori_loop(1,steps,pre,0)
    for t in range(tiles):
        m=jnp.broadcast_to(jnp.max(top[t%2],axis=1,keepdims=True),(G*RT,HW))
        top[t%2]=m
        weigh(t,0,True,m)
        if t+1<tiles: score(t+1,0,True)
        def step(j,_):
            weigh(t,j,False,top[t%2])
            if t+1<tiles: score(t+1,j,False)
            return _
        lax.fori_loop(1,steps,step,0)
        a=acc[...]
        o=(a[:,:HW]/a[:,HW:]).astype(jnp.bfloat16)
        for h in range(G):
            att[t*RT:(t+1)*RT,h*HW:(h+1)*HW]=o[h*RT:(h+1)*RT]
    out_ref[...]=jnp.dot(att[...],w_ref[...],preferred_element_type=jnp.float32).astype(jnp.bfloat16)

def attention(q0,low,q,own,d2,d4,d6,d8,odd,w):
    rows=q.shape[0]
    vm=pl.BlockSpec(memory_space=pltpu.VMEM)
    return pl.pallas_call(
        functools.partial(attention_kernel,q0),
        out_shape=jax.ShapeDtypeStruct((rows,w.shape[1]),jnp.bfloat16),
        in_specs=[pl.BlockSpec(memory_space=pltpu.SMEM)]+[vm]*8,
        out_specs=vm,
        scratch_shapes=[
            pltpu.VMEM((9*512,2*HW),jnp.bfloat16),
            pltpu.VMEM((9*512,2*HW),jnp.bfloat16),
            pltpu.VMEM((2,G*RT,4096),jnp.float32),
            pltpu.VMEM((2,G*RT,HW),jnp.float32),
            pltpu.VMEM((G*RT,2*HW),jnp.float32),
            pltpu.VMEM((rows,G*HW),jnp.bfloat16),
        ],
        compiler_params=pltpu.CompilerParams(vmem_limit_bytes=60<<20),
    )(low,q,own,d2,d4,d6,d8,odd,w)


def mm(a,b):
    return jnp.dot(a.astype(bf),b.astype(bf),preferred_element_type=f32)
def mm_t(a,b):
    return lax.dot_general(a.astype(bf),b.astype(bf),(((1,),(1,)),((),())),preferred_element_type=f32)
def tmm(a,b):
    return lax.dot_general(a.astype(bf),b.astype(bf),(((0,),(0,)),((),())),preferred_element_type=f32)

def delta_kernel(lift_ref, cumr_ref, cumc_ref, lastc_ref, strc_ref, maps_ref, twist_ref, local_ref, mixed_s, red_s, loc_s, tx_s):
    blocks=lift_ref.shape[0]//C
    i=lax.broadcasted_iota(jnp.int32,(W4,W4),0)
    j=lax.broadcasted_iota(jnp.int32,(W4,W4),1)
    within=(i>=j)&(i//C==j//C)
    strict=(i>j)&(i//C==j//C)
    levels=[]
    size=1
    while size<C:
        levels.append((i//(2*size)==j//(2*size))&(i//size!=j//size)&(i>j))
        size*=2
    eye=jnp.where(i==j,1.0,0.0).astype(f32)
    def unit(x):
        return x/jnp.sqrt(jnp.sum(x*x,axis=1,keepdims=True)+1e-6)
    K=[];Q=[];R=[];L=[];A=[]
    for n in range(blocks):
        rows=slice(n*C,(n+1)*C)
        q=unit(lift_ref[rows,:HW]); k=unit(lift_ref[rows,HW:2*HW])
        k4=jnp.concatenate([k]*G,axis=0); q4=jnp.concatenate([q]*G,axis=0)
        v4=jnp.concatenate([lift_ref[rows,(2+h)*HW:(3+h)*HW] for h in range(G)],axis=0)
        cc=cumc_ref[:,n:n+1]; cr=cumr_ref[n:n+1,:]; b=strc_ref[:,n:n+1]
        ratio=jnp.where(within,jnp.exp(jnp.where(within,cc-cr,0.0)),0.0)
        L.append(jnp.where(strict,b*ratio*mm_t(k4,k4),0.0))
        A.append((mm_t(q4,k4)*ratio).astype(bf))
        growth=jnp.exp(cc)
        R.append(jnp.concatenate([(b*growth)*k4,b*v4],axis=1).astype(bf))
        Q.append(growth*q4)
        K.append((jnp.exp(lastc_ref[:,n:n+1]-cc)*k4).astype(bf))
    X=[eye-jnp.where(levels[0],L[n],0.0) for n in range(blocks)]
    for mask in levels[1:]:
        Y=[mm(X[n],jnp.where(mask,L[n],0.0)) for n in range(blocks)]
        X=[X[n]-mm(Y[n],X[n]) for n in range(blocks)]
    M=[mm(X[n],R[n]) for n in range(blocks)]
    S=[mm(A[n],M[n]) for n in range(blocks)]
    state=[None]*G
    ii=lax.broadcasted_iota(jnp.int32,(HW,2*HW),0)
    jj=lax.broadcasted_iota(jnp.int32,(HW,2*HW),1)
    start=jnp.where(ii==jj,1.0,0.0).astype(f32)
    state=[start]*G
    right=jj>=HW
    for n in range(blocks):
        red=Q[n]-S[n][:,:HW]
        for h in range(G):
            hr=slice(h*C,(h+1)*C)
            t=tmm(K[n][hr],M[n][hr])
            last=jnp.exp(lastc_ref[h*C:h*C+1,n:n+1])
            both=mm(jnp.concatenate([red[hr],t[:,:HW]],axis=0),state[h])
            twist_ref[h,n*C:(n+1)*C,:]=both[:C,:HW].astype(bf)
            local_ref[n*C:(n+1)*C,h*HW:(h+1)*HW]=both[:C,HW:]+S[n][hr,HW:]
            state[h]=last*state[h]-both[C:]+jnp.where(right,t,0.0)
    for h in range(G):
        maps_ref[h]=state[h].astype(bf)

def delta_local(lift,cumr,cumc,lastc,strc):
    rows=lift.shape[0]
    vm=pl.BlockSpec(memory_space=pltpu.VMEM)
    return pl.pallas_call(
        delta_kernel,
        out_shape=(jax.ShapeDtypeStruct((G,HW,2*HW),bf),jax.ShapeDtypeStruct((G,rows,HW),bf),jax.ShapeDtypeStruct((rows,G*HW),f32)),
        in_specs=[vm]*5,out_specs=(vm,vm,vm),
        scratch_shapes=[pltpu.VMEM((8,128),f32)]*4,
        compiler_params=pltpu.CompilerParams(vmem_limit_bytes=60<<20),
    )(lift,cumr,cumc,lastc,strc)

def decay_terms(write_strength,log_decay,C=64):
    g,rows=log_decay.shape
    blocks=rows//C
    cum=jnp.cumsum(log_decay.reshape(g,blocks,C),axis=-1)
    last=jnp.broadcast_to(cum[:,:,-1:],cum.shape)
    col=lambda a: a.transpose(0,2,1).reshape(g*C,blocks)
    return (cum.transpose(1,0,2).reshape(blocks,g*C),col(cum),col(last),col(write_strength.reshape(g,blocks,C)))


def spread(before, later):
    high = before.astype(bf)
    low = (before - high.astype(f32)).astype(bf)
    m = later[:, :HW]
    return (jnp.dot(m, high, preferred_element_type=f32)
            + jnp.dot(m, low, preferred_element_type=f32))


def with_injected(before, later):
    n = later[:, HW:].astype(f32)
    return spread(before, later) + jnp.concatenate([jnp.zeros_like(n), n], axis=1)


def chip_kernel(at_ref, own_ref, other_ref, first_ref, total_ref):
    c = at_ref[2]
    for h in range(2):
        own, other = own_ref[2 * c + h], other_ref[h]
        first = jnp.where(c == 0, own, other)
        second = jnp.where(c == 0, other, own)
        first_ref[h] = first
        total_ref[h] = with_injected(first.astype(f32), second).astype(bf)


def row_kernel(at_ref, t0_ref, t1_ref, t2_ref, t3_ref, prefix_ref, total_ref, parts):
    y = at_ref[1]
    for r, t in enumerate((t0_ref, t1_ref, t2_ref, t3_ref)):
        parts[lax.rem(y - r + 4, 4)] = t[...]
    i = lax.broadcasted_iota(jnp.int32, (HW, 2 * HW), 0)
    j = lax.broadcasted_iota(jnp.int32, (HW, 2 * HW), 1)
    start = jnp.where(i == j, 1.0, 0.0).astype(f32)
    for h in range(2):
        now = start
        kept = start
        for k in range(4):
            kept = jnp.where(k == y, now, kept)
            now = with_injected(now, parts[k, h])
        prefix_ref[h] = kept
        total_ref[h] = now.astype(bf)


def column_kernel(at_ref, x1_ref, x2_ref, x3_ref, prefix_ref, first_ref, mine_ref, other_ref):
    x, c = at_ref[0], at_ref[2]
    for h in range(2):
        state = jnp.zeros((HW, HW), f32)
        for d, t in ((3, x3_ref), (2, x2_ref), (1, x1_ref)):
            new = spread(state, t[h]) + t[h, :, HW:].astype(f32)
            state = jnp.where(x >= d, new, state)
        p = prefix_ref[h]
        p_high = p[:, :HW].astype(bf)
        p_low = (p[:, :HW] - p_high.astype(f32)).astype(bf)
        s = state.astype(bf)
        s_low = (state - s.astype(f32)).astype(bf)
        zero = (jnp.dot(p_high, s, preferred_element_type=f32)
                + jnp.dot(p_low, s, preferred_element_type=f32)
                + jnp.dot(p_high, s_low, preferred_element_type=f32) + p[:, HW:])
        one = spread(zero, first_ref[h]) + first_ref[h, :, HW:].astype(f32)
        mine_ref[h] = jnp.where(c == 0, zero, one).astype(bf)
        other_ref[h] = jnp.where(c == 0, one, zero).astype(bf)


def readout_kernel(at_ref, mine_ref, other_ref, twist_ref, local_ref, out_ref):
    c = at_ref[2]
    for h in range(G):
        own = (h // 2) == c
        state = jnp.where(own, mine_ref[h % 2], other_ref[h % 2])
        cols = slice(h * HW, (h + 1) * HW)
        out_ref[:, cols] = (local_ref[:, cols] + jnp.dot(
            twist_ref[h], state, preferred_element_type=f32)).astype(bf)


def norm_kernel(residual_ref, sum_ref, gain_ref, mixed_ref, normed_ref):
    mixed = (residual_ref[...].astype(f32) + sum_ref[...].astype(f32)).astype(bf)
    mixed_ref[...] = mixed
    stream = mixed.astype(f32)
    scale = lax.rsqrt(jnp.mean(stream * stream, axis=-1, keepdims=True) + 1e-06)
    normed_ref[...] = (stream * scale * gain_ref[...]).astype(bf)


VM = pl.BlockSpec(memory_space=pltpu.VMEM)
SM = pl.BlockSpec(memory_space=pltpu.SMEM)


def local_call(kernel, shapes, scalars, *arrays, scratch=()):
    return pl.pallas_call(
        kernel,
        out_shape=shapes,
        in_specs=[SM] * len(scalars) + [VM] * len(arrays),
        out_specs=jax.tree.map(lambda _: VM, shapes),
        scratch_shapes=list(scratch),
        compiler_params=pltpu.CompilerParams(vmem_limit_bytes=48 << 20),
    )(*scalars, *arrays)


def shape(dims, kind=bf):
    return jax.ShapeDtypeStruct(dims, kind)


def rotated(array, axis, by):
    n = lax.axis_size(axis)
    return lax.ppermute(array, axis, [(i, (i + by) % n) for i in range(n)])


def shifted(array, axis, by):
    n = lax.axis_size(axis)
    return lax.ppermute(array, axis, [(i, i + by) for i in range(n - by)])


def earlier_rows(own):
    y, c = lax.axis_index("y"), lax.axis_index("c")
    count = lax.axis_size("y")
    above = shifted(own, "x", 1)
    d = {8: above}
    for r in (1, 2, 3):
        d[2 * r] = rotated(jnp.where(y + r >= count, above, own), "y", r)
    odd = jnp.where(
        c == 0,
        jnp.stack([own, d[2], d[4], d[6]]),
        jnp.stack([d[2], d[4], d[6], d[8]]),
    )
    return d, rotated(odd, "c", 1)


def incoming_state(at, maps):
    c = at[2]
    theirs = rotated(lax.dynamic_slice_in_dim(maps, 2 * (1 - c), 2, 0), "c", 1)
    two = shape((2, HW, 2 * HW))
    first, total = local_call(chip_kernel, (two, two), (at,), maps, theirs)
    parts = [total] + [rotated(total, "y", r) for r in (1, 2, 3)]
    prefix, row = local_call(
        row_kernel, (shape((2, HW, 2 * HW), f32), two), (at,), *parts,
        scratch=[pltpu.VMEM((4, 2, HW, 2 * HW), bf)],
    )
    rows = [shifted(row, "x", d) for d in (1, 2, 3)]
    square = shape((2, HW, HW))
    mine, other = local_call(column_kernel, (square, square), (at,), *rows, prefix, first)
    return mine, rotated(other, "c", 1)


def body(
    residual,
    sliding_query_heads,
    sliding_key_heads,
    sliding_value_heads,
    output_weight,
    norm_gain,
    query_weight,
    key_weight,
    value_weight,
    write_strength,
    log_decay,
):
    x, y, c = (lax.axis_index(a) for a in SEQ)
    at = jnp.stack([x, y, c]).astype(jnp.int32)
    shard = (x * lax.axis_size("y") + y) * 2 + c
    low = jnp.maximum(0, (WINDOW // TOK - shard) * TOK).astype(jnp.int32)[None]
    own = jnp.concatenate([sliding_key_heads, sliding_value_heads], axis=1)
    d, odd = earlier_rows(own)
    weights = jnp.concatenate([query_weight, key_weight, value_weight], axis=1)
    terms = decay_terms(write_strength, log_decay)
    projected = attention(
        0, low, sliding_query_heads, own, d[2], d[4], d[6], d[8], odd, output_weight)
    summed = lax.psum_scatter(projected, "head", scatter_dimension=0, tiled=True)
    mixed_stream, normed = local_call(
        norm_kernel, (shape(residual.shape), shape(residual.shape)), (),
        residual, summed, norm_gain[None, :])
    piece = lax.all_gather(normed, "head", axis=0, tiled=True)
    lifted = jnp.dot(piece, weights, preferred_element_type=f32)
    maps, twisted, local = delta_local(lifted, *terms)
    mine, other = incoming_state(at, maps)
    delta_output = local_call(
        readout_kernel, shape((lifted.shape[0], G * HW)), (at,), mine, other, twisted, local)
    return mixed_stream, delta_output


def solution(mesh):
    devices = mesh.devices.reshape(4, 4, 2, 8)
    split = Mesh(devices, SEQ + ("head",))
    in_specs = (
        P(SEQ + ("head",), None),
        P(SEQ, "head"),
        P(SEQ, "head"),
        P(SEQ, "head"),
        P("head", None),
        P(),
        P(None, "head"),
        P(None, "head"),
        P(None, "head"),
        P("head", SEQ),
        P("head", SEQ),
    )
    out_specs = (P(SEQ + ("head",), None), P(SEQ, "head"))
    return jax.shard_map(body, mesh=split, in_specs=in_specs, out_specs=out_specs, check_vma=False)
```

time: 480 us -> 240 us (0.50)
  matrix products: 174 us -> 8.04 us
  waiting for transfers between devices: 216 us -> 135 us
  Pallas kernels: 0 us -> 43.1 us
  starting transfers between devices: 47.1 us -> 26.6 us
  other arithmetic: 12.4 us -> 1.25 us
    dot_general x221 -> x1, matrix products: 174 us -> 8.04 us  [body(): lifted = jnp.dot(piece, weights, preferred_element_type=f32)]
    all_gather x2 -> x0, waiting for transfers between devices: 102 us -> none  [carried_in(): lax.all_gather(part.astype(kind), axis)]
    pallas_call x0 -> x7, Pallas kernels: none -> 43.1 us  [the longest x1 24.9 us: attention(): pl.pallas_call(functools.partial(attention_kernel, q0), out_shape=jax.Sha...]
    ppermute x16 -> x13, waiting for transfers between devices: 2.39 us -> 26.2 us  [the longest x9 18.3 us: rotated(): return lax.ppermute(array, axis, [(i, (i + by) % n) for i in range(n)])]
    ppermute x16 -> x13, starting transfers between devices: 46.7 us -> 26.3 us  [the longest x9 14.9 us: rotated(): return lax.ppermute(array, axis, [(i, (i + by) % n) for i in range(n)])]
    reduce_sum x5 -> x0, other arithmetic: 6.95 us -> none  [the longest x4 5.62 us: one_head(): jnp.sum(weights, axis=-1, keepdims=True)]
  transfers between devices with their start and end apart: 20 -> 15, of which waited for: 6 -> 11; matrix products, arithmetic and copies ran while one was open for 1% -> 1% of each run, Pallas kernels for 0% -> 0%
where the time goes in v1:
time: 240 us; the launch traced here: 239 us
  waiting for transfers between devices  135 us (56%)
  Pallas kernels  43.1 us (18%)
  starting transfers between devices  26.6 us (11%)
  between operations  14.2 us (6%)
  local copies, waits for them, and re-layouts  11.2 us (5%)
  matrix products  8.04 us (3%)
    reduce_scatter x1, waiting for transfers between devices, body(): lax.psum_scatter(projected, 'head', scatter_dimension=0, tiled=True)  58.3 us
    all_gather x1, waiting for transfers between devices, body(): piece = lax.all_gather(normed, 'head', axis=0, tiled=True)  50.1 us
    pallas_call x1, Pallas kernels, attention(): pl.pallas_call(functools.partial(attention_kernel, q0), out_shape=jax.Sha...  24.9 us
    ppermute x9, waiting for transfers between devices, rotated(): return lax.ppermute(array, axis, [(i, (i + by) % n) for i in range(n)])  18.3 us
    ppermute x9, starting transfers between devices, rotated(): return lax.ppermute(array, axis, [(i, (i + by) % n) for i in range(n)])  14.9 us
    ppermute x4, starting transfers between devices, shifted(): return lax.ppermute(array, axis, [(i, i + by) for i in range(n - by)])  11.5 us
    pallas_call x1, Pallas kernels, delta_local(): pl.pallas_call(delta_kernel, out_shape=(jax.ShapeDtypeStruct((G, HW, 2 *...  10.9 us
    dot_general x1, matrix products, body(): lifted = jnp.dot(piece, weights, preferred_element_type=f32)  8.04 us
  transfers between devices with their start and end apart: 15, of which 11 were waited for; matrix products, arithmetic and copies ran while one was open for 1% of the time, Pallas kernels for 0%

profile of v1, /device:TPU:1, one launch (start us, length us, event | category | flops | bytes accessed | tf_op | source)
XLA Modules:
  0.0 239.1 jit_solution(12739244678989914391)
XLA Ops:
  7.2 0.0 reduce-scatter.2.cloned.1.call-start
  7.2 0.9 constant_dynamic-update-slice_fusion.1
  8.1 0.9 constant_dynamic-update-slice_fusion.own_ref
  9.1 0.0 copy-start.6
  9.1 4.0 %collective-permute-start = (bf16[512,256]{1,0:T(8,128)(2,1)S(1)}, bf16[512,256]{1,0:T(8,128)(2,1)S(1)}, u32[]{:S(2)}, u32[]{:S(2)}) collective-permute-start(bf16[512,256]{1,0:T(8,128)(2,1)S(1)} %constant_dynamic-update-slice_fusion.own_ref), channel_id=1, source_target_pairs={{0,64},{64,128},{128,192},{1,65},{65,129},{129,193},{2,66},{66,130... | collective-permute-start | bytes 786440 | tf_op jit(solution)/shard_map/ppermute | solution.py:310
  13.1 4.9 %collective-permute-done.d8_ref = bf16[512,256]{1,0:T(8,128)(2,1)S(1)} collective-permute-done((bf16[512,256]{1,0:T(8,128)(2,1)S(1)}, bf16[512,256]{1,0:T(8,128)(2,1)S(1)}, u32[]{:S(2)}, u32[]{:S(2)}) %collective-permute-start) | collective-permute-done | bytes 262176 | tf_op jit(solution)/shard_map/ppermute | solution.py:310
  18.0 0.1 broadcast_select_fusion
  18.1 1.4 collective-permute-start.1
  19.4 2.6 %collective-permute-start.2 = (bf16[512,256]{1,0:T(8,128)(2,1)S(1)}, bf16[512,256]{1,0:T(8,128)(2,1)S(1)}, u32[]{:S(2)}, u32[]{:S(2)}) collective-permute-start(bf16[512,256]{1,0:T(8,128)(2,1)S(1)} %get-tuple-element.25), channel_id=1, source_target_pairs={{0,32},{16,48},{32,0},{48,16},{1,33},{17,49},{33,1},{49,17},{2,34}... | collective-permute-start | bytes 786440 | tf_op jit(solution)/shard_map/ppermute | solution.py:305
  22.1 1.1 collective-permute-start.3
  23.1 2.6 %collective-permute-done.1.d2_ref = bf16[512,256]{1,0:T(8,128)(2,1)S(1)} collective-permute-done((bf16[512,256]{1,0:T(8,128)(2,1)S(1)}, bf16[512,256]{1,0:T(8,128)(2,1)S(1)}, u32[]{:S(2)}, u32[]{:S(2)}) %collective-permute-start.1) | collective-permute-done | bytes 262176 | tf_op jit(solution)/shard_map/ppermute | solution.py:305
  25.7 6.7 %collective-permute-done.2.d4_ref = bf16[512,256]{1,0:T(8,128)(2,1)S(1)} collective-permute-done((bf16[512,256]{1,0:T(8,128)(2,1)S(1)}, bf16[512,256]{1,0:T(8,128)(2,1)S(1)}, u32[]{:S(2)}, u32[]{:S(2)}) %collective-permute-start.2) | collective-permute-done | bytes 262176 | tf_op jit(solution)/shard_map/ppermute | solution.py:305
  32.5 0.0 collective-permute-done.3.d6_ref
  32.5 0.2 maximum_select_fusion
  32.7 2.6 %collective-permute-start.4 = (bf16[4,512,256]{2,1,0:T(8,128)(2,1)S(1)}, bf16[4,512,256]{2,1,0:T(8,128)(2,1)S(1)}, u32[]{:S(2)}, u32[]{:S(2)}) collective-permute-start(bf16[4,512,256]{2,1,0:T(8,128)(2,1)S(1)} %maximum_select_fusion), channel_id=1, source_target_pairs={{0,8},{8,0},{1,9},{9,1},{2,10},{10,2},{3,11},{11,3},{4,12},{12,4},... | collective-permute-start | bytes 3145736 | tf_op jit(solution)/shard_map/ppermute | solution.py:305
  35.3 2.3 collective-permute-done.4.odd_ref
  37.6 0.0 copy-done.9
  37.6 1.0 copy-done.11
  38.6 24.9 %shard_map.122 = bf16[512,4096]{1,0:T(8,128)(2,1)} custom-call(s32[1]{0:T(128)} %bitcast.low_ref, bf16[512,512]{1,0:T(8,128)(2,1)} %q_ref.1, bf16[512,256]{1,0:T(8,128)(2,1)} %copy-done.6, bf16[512,256]{1,0:T(8,128)(2,1)} %copy-done.8, bf16[512,256]{1,0:T(8,128)(2,1)} %copy-done.9, bf16[512,256]{1,0:T(8,128)(2,1)} %copy-done.10, bf16[512,256]{1,0:T(8,128)(2,1)} %copy-done.7, ...), custom_call_target="tpu_custom_call" | custom-call | tf_op jit(solution)/shard_map/pallas_call | solution.py:109
  63.5 0.0 copy-start.13
  63.5 0.0 copy-start.14
  63.5 0.0 copy-start.15
  63.5 0.0 reduce-scatter.2.cloned.1.call-update
  63.6 0.2 all-gather.2.cloned.1.call-start
  63.8 58.3 %reduce-scatter.2.cloned.1.call-done.sum_ref = bf16[64,4096]{1,0:T(8,128)(2,1)} async-done(((bf16[512,4096]{1,0:T(8,128)(2,1)}), bf16[64,4096]{1,0:T(8,128)(2,1)}) %reduce-scatter.2.cloned.1.call-update) | async-done | bytes 524304 | tf_op jit(solution)/shard_map/reduce_scatter | solution.py:367
  122.1 1.0 copy-done.4
  123.2 1.2 shard_map.123
  124.4 0.0 all-gather.2.cloned.1.call-update
  124.4 0.1 reshape.22
  124.5 0.9 reduce_window_sum.11
  125.4 0.8 copy.17
  126.2 0.7 reshape.23.cumr_ref
  126.8 0.1 reshape.26
  126.9 0.8 copy.18
  127.7 0.2 slice_reduce_fusion
  127.8 50.1 %all-gather.2.cloned.1.call-done = bf16[512,4096]{1,0:T(8,128)(2,1)} async-done(((bf16[64,4096]{1,0:T(8,128)(2,1)}), bf16[512,4096]{1,0:T(8,128)(2,1)}) %all-gather.2.cloned.1.call-update) | async-done | bytes 4194320 | tf_op jit(solution)/shard_map/all_gather | solution.py:371
  178.0 8.0 %fusion.lift_ref = f32[512,768]{1,0:T(8,128)} fusion(bf16[512,4096]{1,0:T(8,128)(2,1)} %all-gather.2.cloned.1.call-done, bf16[4096,512]{1,0:T(8,128)(2,1)} %param.19, bf16[4096,128]{1,0:T(8,128)(2,1)S(1)} %copy-done.14, bf16[4096,128]{1,0:T(8,128)(2,1)S(1)} %copy-done.15), kind=kOutput, calls=%fused_computation | convolution fusion | flops 3240099840 | bytes 12058624 | tf_op jit(solution)/shard_map/dot_general | solution.py:372
  186.0 0.7 transpose.15
  186.7 10.9 %shard_map.124 = (bf16[4,128,256]{2,1,0:T(8,128)(2,1)}, bf16[4,512,128]{2,1,0:T(8,128)(2,1)}, f32[512,512]{1,0:T(8,128)}) custom-call(f32[512,768]{1,0:T(8,128)} %fusion.lift_ref, f32[8,256]{1,0:T(8,128)} %reshape.23.cumr_ref, f32[256,8]{1,0:T(8,128)} %bitcast.24, f32[256,8]{1,0:T(8,128)} %bitcast.26, f32[256,8]{1,0:T(8,128)} %bitcast.25), custom_call_target="tpu_custom_call" | custom-call | tf_op jit(solution)/shard_map/pallas_call | solution.py:189
  197.6 0.9 constant_dynamic-slice_fusion
  198.5 0.8 collective-permute-start.5
  199.3 0.1 pad_add_fusion.at_ref
  199.4 0.9 collective-permute-done.5.other_ref
  200.3 0.9 copy-done.1
  201.2 0.8 shard_map.125
  202.0 1.5 collective-permute-start.6
  203.5 2.4 %collective-permute-start.7 = (bf16[2,128,256]{2,1,0:T(8,128)(2,1)S(1)}, bf16[2,128,256]{2,1,0:T(8,128)(2,1)S(1)}, u32[]{:S(2)}, u32[]{:S(2)}) collective-permute-start(bf16[2,128,256]{2,1,0:T(8,128)(2,1)S(1)} %get-tuple-element.16.t0_ref), channel_id=1, source_target_pairs={{0,32},{16,48},{32,0},{48,16},{1,33},{17,49},{33,1},{49,17},{2,34}... | collective-permute-start | bytes 393224 | tf_op jit(solution)/shard_map/ppermute | solution.py:305
  205.9 1.2 collective-permute-start.8
  207.1 1.1 collective-permute-done.6.t1_ref
  208.2 3.8 %collective-permute-done.7.t2_ref = bf16[2,128,256]{2,1,0:T(8,128)(2,1)S(1)} collective-permute-done((bf16[2,128,256]{2,1,0:T(8,128)(2,1)S(1)}, bf16[2,128,256]{2,1,0:T(8,128)(2,1)S(1)}, u32[]{:S(2)}, u32[]{:S(2)}) %collective-permute-start.7) | collective-permute-done | bytes 131104 | tf_op jit(solution)/shard_map/ppermute | solution.py:305
  212.0 0.0 collective-permute-done.8.t3_ref
  212.0 1.7 shard_map.126
  213.8 4.6 %collective-permute-start.10 = (bf16[2,128,256]{2,1,0:T(8,128)(2,1)S(1)}, bf16[2,128,256]{2,1,0:T(8,128)(2,1)S(1)}, u32[]{:S(2)}, u32[]{:S(2)}) collective-permute-start(bf16[2,128,256]{2,1,0:T(8,128)(2,1)S(1)} %get-tuple-element.17), channel_id=1, source_target_pairs={{0,128},{64,192},{1,129},{65,193},{2,130},{66,194},{3,131},{67,195... | collective-permute-start | bytes 393224 | tf_op jit(solution)/shard_map/ppermute | solution.py:310
  218.4 1.3 collective-permute-start.11
  219.7 1.6 collective-permute-start.9
  221.3 0.0 collective-permute-done.10.x2_ref
  221.3 2.9 %collective-permute-done.11.x3_ref = bf16[2,128,256]{2,1,0:T(8,128)(2,1)S(1)} collective-permute-done((bf16[2,128,256]{2,1,0:T(8,128)(2,1)S(1)}, bf16[2,128,256]{2,1,0:T(8,128)(2,1)S(1)}, u32[]{:S(2)}, u32[]{:S(2)}) %collective-permute-start.11) | collective-permute-done | bytes 131104 | tf_op jit(solution)/shard_map/ppermute | solution.py:310
  224.2 0.0 collective-permute-done.9.x1_ref
  224.2 1.8 shard_map.127
  226.1 1.4 collective-permute-start.12
  227.5 0.9 collective-permute-done.12.other_ref
  228.4 1.2 copy-done
  229.6 1.0 copy-done.2
  230.6 1.6 shard_map.128
  (23 shorter events, 0.0 us)
Async XLA Ops:
  7.2 115.0 %reduce-scatter.2.cloned.1.call-start = ((), (), s32[]{:S(2)}) async-start(), calls=%async_computation.1 | async-start | bytes 4718592 | tf_op jit(solution)/shard_map/reduce_scatter | solution.py:367
  9.1 28.5 %copy-start.6 = (bf16[512,256]{1,0:T(8,128)(2,1)}, bf16[512,256]{1,0:T(8,128)(2,1)S(1)}, u32[]{:S(2)}) copy-start(bf16[512,256]{1,0:T(8,128)(2,1)S(1)} %constant_dynamic-update-slice_fusion.own_ref) | copy-start | bytes 786436
  9.1 8.9 %collective-permute-start = (bf16[512,256]{1,0:T(8,128)(2,1)S(1)}, bf16[512,256]{1,0:T(8,128)(2,1)S(1)}, u32[]{:S(2)}, u32[]{:S(2)}) collective-permute-start(bf16[512,256]{1,0:T(8,128)(2,1)S(1)} %constant_dynamic-update-slice_fusion.own_ref), channel_id=1, source_target_pairs={{0,64},{64,128},{128,192},{1,65},{65,129},{129,193},{2,66},{66,130... | collective-permute-start | bytes 786440 | tf_op jit(solution)/shard_map/ppermute | solution.py:310
  18.0 19.6 %copy-start.7 = (bf16[512,256]{1,0:T(8,128)(2,1)}, bf16[512,256]{1,0:T(8,128)(2,1)S(1)}, u32[]{:S(2)}) copy-start(bf16[512,256]{1,0:T(8,128)(2,1)S(1)} %collective-permute-done.d8_ref) | copy-start | bytes 786436
  18.1 7.7 %collective-permute-start.1 = (bf16[512,256]{1,0:T(8,128)(2,1)S(1)}, bf16[512,256]{1,0:T(8,128)(2,1)S(1)}, u32[]{:S(2)}, u32[]{:S(2)}) collective-permute-start(bf16[512,256]{1,0:T(8,128)(2,1)S(1)} %get-tuple-element.26), channel_id=1, source_target_pairs={{0,16},{16,32},{32,48},{48,0},{1,17},{17,33},{33,49},{49,1},{2,18}... | collective-permute-start | bytes 786440 | tf_op jit(solution)/shard_map/ppermute | solution.py:305
  19.4 13.0 %collective-permute-start.2 = (bf16[512,256]{1,0:T(8,128)(2,1)S(1)}, bf16[512,256]{1,0:T(8,128)(2,1)S(1)}, u32[]{:S(2)}, u32[]{:S(2)}) collective-permute-start(bf16[512,256]{1,0:T(8,128)(2,1)S(1)} %get-tuple-element.25), channel_id=1, source_target_pairs={{0,32},{16,48},{32,0},{48,16},{1,33},{17,49},{33,1},{49,17},{2,34}... | collective-permute-start | bytes 786440 | tf_op jit(solution)/shard_map/ppermute | solution.py:305
  22.1 10.4 %collective-permute-start.3 = (bf16[512,256]{1,0:T(8,128)(2,1)S(1)}, bf16[512,256]{1,0:T(8,128)(2,1)S(1)}, u32[]{:S(2)}, u32[]{:S(2)}) collective-permute-start(bf16[512,256]{1,0:T(8,128)(2,1)S(1)} %get-tuple-element.24), channel_id=1, source_target_pairs={{0,48},{16,0},{32,16},{48,32},{1,49},{17,1},{33,17},{49,33},{2,50}... | collective-permute-start | bytes 786440 | tf_op jit(solution)/shard_map/ppermute | solution.py:305
  25.7 11.8 %copy-start.8 = (bf16[512,256]{1,0:T(8,128)(2,1)}, bf16[512,256]{1,0:T(8,128)(2,1)S(1)}, u32[]{:S(2)}) copy-start(bf16[512,256]{1,0:T(8,128)(2,1)S(1)} %collective-permute-done.1.d2_ref) | copy-start | bytes 786436
  32.5 5.1 %copy-start.9 = (bf16[512,256]{1,0:T(8,128)(2,1)}, bf16[512,256]{1,0:T(8,128)(2,1)S(1)}, u32[]{:S(2)}) copy-start(bf16[512,256]{1,0:T(8,128)(2,1)S(1)} %collective-permute-done.2.d4_ref) | copy-start | bytes 786436
  32.5 5.1 %copy-start.10 = (bf16[512,256]{1,0:T(8,128)(2,1)}, bf16[512,256]{1,0:T(8,128)(2,1)S(1)}, u32[]{:S(2)}) copy-start(bf16[512,256]{1,0:T(8,128)(2,1)S(1)} %collective-permute-done.3.d6_ref) | copy-start | bytes 786436
  32.7 4.8 %collective-permute-start.4 = (bf16[4,512,256]{2,1,0:T(8,128)(2,1)S(1)}, bf16[4,512,256]{2,1,0:T(8,128)(2,1)S(1)}, u32[]{:S(2)}, u32[]{:S(2)}) collective-permute-start(bf16[4,512,256]{2,1,0:T(8,128)(2,1)S(1)} %maximum_select_fusion), channel_id=1, source_target_pairs={{0,8},{8,0},{1,9},{9,1},{2,10},{10,2},{3,11},{11,3},{4,12},{12,4},... | collective-permute-start | bytes 3145736 | tf_op jit(solution)/shard_map/ppermute | solution.py:305
  37.6 1.0 copy-start.11
  63.5 58.6 %copy-start.3 = (bf16[64,4096]{1,0:T(8,128)(2,1)S(1)}, bf16[64,4096]{1,0:T(8,128)(2,1)}, u32[]{:S(2)}) copy-start(bf16[64,4096]{1,0:T(8,128)(2,1)} %residual_ref.1) | copy-start | bytes 1572868
  63.5 58.6 %copy-start.5 = (f32[4096]{0:T(1024)S(1)}, f32[4096]{0:T(1024)}, u32[]{:S(2)}) copy-start(f32[4096]{0:T(1024)} %param.16) | copy-start | bytes 49156
  63.5 60.9 %copy-start.12 = (f32[4,512]{1,0:T(4,128)S(1)}, f32[4,512]{1,0:T(4,128)}, u32[]{:S(2)}) copy-start(f32[4,512]{1,0:T(4,128)} %param.21) | copy-start | bytes 24580
  63.5 63.3 %copy-start.13 = (f32[4,512]{1,0:T(4,128)S(1)}, f32[4,512]{1,0:T(4,128)}, u32[]{:S(2)}) copy-start(f32[4,512]{1,0:T(4,128)} %param.20) | copy-start | bytes 24580
  63.5 114.5 %copy-start.14 = (bf16[4096,128]{1,0:T(8,128)(2,1)S(1)}, bf16[4096,128]{1,0:T(8,128)(2,1)}, u32[]{:S(2)}) copy-start(bf16[4096,128]{1,0:T(8,128)(2,1)} %param.18) | copy-start | bytes 3145732
  63.5 114.4 %copy-start.15 = (bf16[4096,128]{1,0:T(8,128)(2,1)S(1)}, bf16[4096,128]{1,0:T(8,128)(2,1)}, u32[]{:S(2)}) copy-start(bf16[4096,128]{1,0:T(8,128)(2,1)} %param.17) | copy-start | bytes 3145732
  63.6 114.4 %all-gather.2.cloned.1.call-start = ((), (), s32[]{:S(2)}) async-start(), calls=%async_computation.2 | async-start | bytes 4718592 | tf_op jit(solution)/shard_map/all_gather | solution.py:371
  122.1 1.0 copy-start.4
  198.5 1.7 collective-permute-start.5
  200.3 0.9 copy-start.1
  202.0 6.2 %collective-permute-start.6 = (bf16[2,128,256]{2,1,0:T(8,128)(2,1)S(1)}, bf16[2,128,256]{2,1,0:T(8,128)(2,1)S(1)}, u32[]{:S(2)}, u32[]{:S(2)}) collective-permute-start(bf16[2,128,256]{2,1,0:T(8,128)(2,1)S(1)} %get-tuple-element.16.t0_ref), channel_id=1, source_target_pairs={{0,16},{16,32},{32,48},{48,0},{1,17},{17,33},{33,49},{49,1},{2,18}... | collective-permute-start | bytes 393224 | tf_op jit(solution)/shard_map/ppermute | solution.py:305
  203.5 8.5 %collective-permute-start.7 = (bf16[2,128,256]{2,1,0:T(8,128)(2,1)S(1)}, bf16[2,128,256]{2,1,0:T(8,128)(2,1)S(1)}, u32[]{:S(2)}, u32[]{:S(2)}) collective-permute-start(bf16[2,128,256]{2,1,0:T(8,128)(2,1)S(1)} %get-tuple-element.16.t0_ref), channel_id=1, source_target_pairs={{0,32},{16,48},{32,0},{48,16},{1,33},{17,49},{33,1},{49,17},{2,34}... | collective-permute-start | bytes 393224 | tf_op jit(solution)/shard_map/ppermute | solution.py:305
  205.9 6.1 %collective-permute-start.8 = (bf16[2,128,256]{2,1,0:T(8,128)(2,1)S(1)}, bf16[2,128,256]{2,1,0:T(8,128)(2,1)S(1)}, u32[]{:S(2)}, u32[]{:S(2)}) collective-permute-start(bf16[2,128,256]{2,1,0:T(8,128)(2,1)S(1)} %get-tuple-element.16.t0_ref), channel_id=1, source_target_pairs={{0,48},{16,0},{32,16},{48,32},{1,49},{17,1},{33,17},{49,33},{2,50}... | collective-permute-start | bytes 393224 | tf_op jit(solution)/shard_map/ppermute | solution.py:305
  213.8 7.5 %collective-permute-start.10 = (bf16[2,128,256]{2,1,0:T(8,128)(2,1)S(1)}, bf16[2,128,256]{2,1,0:T(8,128)(2,1)S(1)}, u32[]{:S(2)}, u32[]{:S(2)}) collective-permute-start(bf16[2,128,256]{2,1,0:T(8,128)(2,1)S(1)} %get-tuple-element.17), channel_id=1, source_target_pairs={{0,128},{64,192},{1,129},{65,193},{2,130},{66,194},{3,131},{67,195... | collective-permute-start | bytes 393224 | tf_op jit(solution)/shard_map/ppermute | solution.py:310
  218.4 5.8 %collective-permute-start.11 = (bf16[2,128,256]{2,1,0:T(8,128)(2,1)S(1)}, bf16[2,128,256]{2,1,0:T(8,128)(2,1)S(1)}, u32[]{:S(2)}, u32[]{:S(2)}) collective-permute-start(bf16[2,128,256]{2,1,0:T(8,128)(2,1)S(1)} %get-tuple-element.17), channel_id=1, source_target_pairs={{0,192},{1,193},{2,194},{3,195},{4,196},{5,197},{6,198},{7,199},{8... | collective-permute-start | bytes 393224 | tf_op jit(solution)/shard_map/ppermute | solution.py:310
  219.7 4.5 %collective-permute-start.9 = (bf16[2,128,256]{2,1,0:T(8,128)(2,1)S(1)}, bf16[2,128,256]{2,1,0:T(8,128)(2,1)S(1)}, u32[]{:S(2)}, u32[]{:S(2)}) collective-permute-start(bf16[2,128,256]{2,1,0:T(8,128)(2,1)S(1)} %get-tuple-element.17), channel_id=1, source_target_pairs={{0,64},{64,128},{128,192},{1,65},{65,129},{129,193},{2,66},{66,130... | collective-permute-start | bytes 393224 | tf_op jit(solution)/shard_map/ppermute | solution.py:310
  226.1 2.3 collective-permute-start.12
  228.4 1.2 copy-start
  229.6 1.0 copy-start.2
Sparse Core Ops, SparseCore 0:
  63.7 58.3 reduce-scatter.1
  124.6 53.3 all-gather.1
